TPU v7x, 32 devices: a whole 2x2x4 slice. The times are simulated.
32 devices in a mesh: row: 2 (over x), col: 4 (over y, core), rep: 4 (over z).
Axes of the slice: x: 2, y: 2, z: 4, core: 2. Of those that a mesh axis runs over, the one named last changes fastest.
Arguments:
- integrals: bfloat16 [8, 4, 60, 128, 128], P(None, 'row', 'rep', 'col'), may hold values from -0.0625 to 0.0625
- amplitudes: bfloat16 [8, 16, 60, 128, 128], P(None, 'col', 'rep', 'row'), may hold values from -6 to 6
- virt_count: int32 [8], replicated, may hold values from 76 to 128, as said below
- occ_irrep: int32 [60], replicated, may hold values from 0 to 7
Outputs:
- cycle: bfloat16 [8, 4, 128, 16, 128], P('rep', 'row', None, 'col')
Inputs may be any that keep to these rules, and one draw needn't show every extreme that they name: `virt_count`: one irrep has exactly 128 virtual orbitals.
All inputs are finite; a program needn't handle non-finite values.
Results may differ from a plain program's by a relative error of at most 0.001.
Values may be sent and summed in bfloat16 or wider, within the bound.
A program may use at most 128 MiB of HBM per device.

v0:
```python
import jax
import jax.numpy as jnp
from jax import lax
from jax.sharding import PartitionSpec as P


def contract(w_part, t_part):
    w_full = lax.all_gather(w_part, "col", axis=3, tiled=True)
    return jnp.einsum(
        "gikca,gjkcb->giajb",
        w_full,
        lax.all_gather(t_part, "row", axis=3, tiled=True),
        preferred_element_type=jnp.float32,
    )


def body(integrals, amplitudes, virt_count, occ_irrep):
    ngroup = integrals.shape[0]
    k_local = integrals.shape[2]
    c_local = integrals.shape[3]
    nvirt = integrals.shape[4]
    rep_index = lax.axis_index("rep")
    col_index = lax.axis_index("col")
    occ_local = lax.dynamic_slice_in_dim(occ_irrep, rep_index * k_local, k_local)
    groups = jnp.arange(ngroup, dtype=jnp.int32)
    blocks = jnp.bitwise_xor(groups[:, None], occ_local[None, :])
    onehot = blocks[:, :, None] == groups[None, None, :]
    limit = jnp.sum(jnp.where(onehot, virt_count[None, None, :], 0), axis=2)
    c_global = col_index * c_local + jnp.arange(c_local, dtype=jnp.int32)
    c_live = c_global[None, None, :] < limit[:, :, None]
    places = jnp.arange(nvirt, dtype=jnp.int32)
    a_live = places[None, :] < virt_count[:, None]
    keep = c_live[:, None, :, :, None] & a_live[:, None, None, None, :]
    masked = jnp.where(keep, integrals, jnp.zeros_like(integrals))
    owned = ngroup // lax.axis_size("rep")
    partial_cycle = contract(masked, amplitudes)
    summed = lax.psum_scatter(partial_cycle, "rep", scatter_dimension=0, tiled=True)
    own_counts = lax.dynamic_slice_in_dim(virt_count, rep_index * owned, owned)
    b_live = places[None, :] < own_counts[:, None]
    result = jnp.where(b_live[:, None, None, None, :], summed, jnp.zeros_like(summed))
    return result.astype(jnp.bfloat16)


def solution(mesh):
    return jax.shard_map(
        body,
        mesh=mesh,
        in_specs=(P(None, "row", "rep", "col", None), P(None, "col", "rep", "row", None), P(), P()),
        out_specs=P("rep", "row", None, "col", None),
        check_vma=False,
    )
```

profile of v0, /device:TPU:0, one launch (start us, length us, event | category | flops | bytes accessed | tf_op | source)
XLA Modules:
  0.0 359.9 jit_solution(10628862864459718682)
XLA Ops:
  6.5 0.0 all-gather.3.cloned.1.call-start
  6.5 0.7 iota_compare_fusion.1
  7.3 0.7 dynamic_slice.7
  8.0 0.7 select_reduce_fusion
  8.7 0.1 broadcast_compare_fusion
  8.8 0.8 broadcast_and_fusion
  9.6 3.1 broadcast_select_fusion
  12.7 0.0 all-gather.3.cloned.1.call-update
  12.8 0.0 all-gather.5.cloned.1.call-start
  12.8 0.7 all-gather.5.cloned.1.call-update
  13.5 0.0 copy-start
  13.5 0.0 reduce-scatter.2.cloned.1.call-start
  13.6 57.4 %all-gather.3.cloned.1.call-done = bf16[8,2,15,128,128]{4,3,2,1,0:T(8,128)(2,1)} async-done(((bf16[8,2,15,32,128]{4,3,2,1,0:T(8,128)(2,1)}), bf16[8,2,15,128,128]{4,3,2,1,0:T(8,128)(2,1)}) %all-gather.3.cloned.1.call-update) | async-done | bytes 7864336 | tf_op jit(solution)/shard_map/all_gather | solution.py:8
  70.9 188.6 %all-gather.5.cloned.1.call-done = bf16[8,4,15,128,128]{4,3,2,1,0:T(8,128)(2,1)} async-done(((bf16[8,4,15,64,128]{4,3,2,1,0:T(8,128)(2,1)}), bf16[8,4,15,128,128]{4,3,2,1,0:T(8,128)(2,1)}) %all-gather.5.cloned.1.call-update) | async-done | bytes 15728656 | tf_op jit(solution)/shard_map/all_gather | solution.py:12
  259.6 14.3 %fusion.3 = f32[8,2,128,4,128]{4,2,3,1,0:T(8,128)} fusion(bf16[8,4,15,128,128]{4,3,2,1,0:T(8,128)(2,1)} %all-gather.5.cloned.1.call-done, bf16[8,2,15,128,128]{4,3,2,1,0:T(8,128)(2,1)} %all-gather.3.cloned.1.call-done), kind=kOutput, calls=%fused_computation.3 | convolution fusion | flops 4026531840 | bytes 27787264 | tf_op jit(solution)/shard_map/gikca,gjkcb->giajb/dot_general | solution.py:9
  273.9 0.0 reduce-scatter.2.cloned.1.call-update
  273.9 0.0 copy-done
  273.9 0.1 dynamic_slice.6
  274.0 0.1 iota_compare_fusion.2
  274.1 76.8 %reduce-scatter.2.cloned.1.call-done = f32[2,2,128,4,128]{4,2,3,1,0:T(8,128)} async-done(((f32[8,2,128,4,128]{4,2,3,1,0:T(8,128)}), f32[2,2,128,4,128]{4,2,3,1,0:T(8,128)}) %reduce-scatter.2.cloned.1.call-update) | async-done | bytes 1048592 | tf_op jit(solution)/shard_map/reduce_scatter | solution.py:37
  350.8 1.3 select_convert_fusion
  352.2 1.2 copy.6
  (2 shorter events, 0.0 us)
Async XLA Ops:
  6.5 64.4 %all-gather.3.cloned.1.call-start = ((), (), s32[]{:S(2)}) async-start(), calls=%async_computation.1 | async-start | bytes 9830400 | tf_op jit(solution)/shard_map/all_gather | solution.py:8
  12.8 246.8 %all-gather.5.cloned.1.call-start = ((), (), s32[]{:S(2)}) async-start(), calls=%async_computation.2 | async-start | bytes 23592960 | tf_op jit(solution)/shard_map/all_gather | solution.py:12
  13.5 260.4 %copy-start = (s32[8]{0:T(128)S(1)}, s32[8]{0:T(128)}, u32[]{:S(2)}) copy-start(s32[8]{0:T(128)} %param.6) | copy-start | bytes 100
  13.5 337.3 %reduce-scatter.2.cloned.1.call-start = ((), (), s32[]{:S(2)}) async-start(), calls=%async_computation.3 | async-start | bytes 5242880 | tf_op jit(solution)/shard_map/reduce_scatter | solution.py:37
Sparse Core Ops, SparseCore 0:
  12.9 57.9 all-gather.2
  72.5 187.0 all-gather.4
  274.0 76.7 reduce-scatter.1
where the time goes:
time: 360 us
  waiting for transfers between devices  323 us (90%)
  matrix products  14.3 us (4%)
  between operations  13.2 us (4%)
  other arithmetic  6.86 us (2%)
    all_gather x1, waiting for transfers between devices, contract(): lax.all_gather(t_part, 'row', axis=3, tiled=True)  189 us
    reduce_scatter x1, waiting for transfers between devices, body(): lax.psum_scatter(partial_cycle, 'rep', scatter_dimension=0, tiled=True)  76.8 us
    all_gather x1, waiting for transfers between devices, contract(): w_full = lax.all_gather(w_part, 'col', axis=3, tiled=True)  57.4 us
    dot_general x1, matrix products, contract(): jnp.einsum('gikca,gjkcb->giajb', w_full, lax.all_gather(t_part, 'row', ax...  14.3 us
  transfers between devices with their start and end apart: 3, of which 3 were waited for; matrix products, arithmetic and copies ran while one was open for 0% of the time, Pallas kernels for 0%

commit v1 on v0

--- a/solution.py
+++ b/solution.py
@@ -1,7 +1,15 @@
+import functools
+
 import jax
 import jax.numpy as jnp
 from jax import lax
+from jax.experimental import pallas as pl
+from jax.experimental.pallas import tpu as pltpu
 from jax.sharding import PartitionSpec as P
+
+MESH = pl.DeviceIdType.MESH
+TOP = 32767.0
+PAD = 16
 
 
 def contract(w_part, t_part):
@@ -14,11 +22,233 @@
     )
 
 
+def quantise(value, ref):
+    rows = value.shape[0]
+    most = jnp.max(jnp.abs(value), axis=0, keepdims=True)
+    code = jnp.ceil(8.0 * jnp.log2(jnp.maximum(most, 1e-30)))
+    scaled = jnp.clip(jnp.round(value * (jnp.exp2(code * -0.125) * TOP)), -TOP, TOP)
+    ref[0:rows, :] = scaled.astype(jnp.int32).astype(jnp.int16)
+    wide = jnp.broadcast_to(code, (PAD, value.shape[1]))
+    ref[rows : rows + PAD, :] = wide.astype(jnp.int32).astype(jnp.int16)
+
+
+def dequantise(ref):
+    rows = ref.shape[0] - PAD
+    code = ref[rows : rows + PAD, :].astype(jnp.int32).astype(jnp.float32)[0:1, :]
+    return ref[0:rows, :].astype(jnp.int32).astype(jnp.float32) * (jnp.exp2(code * 0.125) * (1.0 / TOP))
+
+
+def kernel(nz, w_ref, t_ref, o_ref, wv, tv, st, pown, xs, xr, zs, zr,
+           t_sem, l_sem, s1, s2, sc, sx, sz, r_own, r_oth, r_st, r_c, r_x, r_z):
+    ng, nk, cw, m = w_ref.shape
+    nj, nb = t_ref.shape[1], t_ref.shape[4]
+    n = nj * nb
+    depth = nk * 2 * cw
+    gz = ng // nz
+    x, col, z = lax.axis_index("row"), lax.axis_index("col"), lax.axis_index("rep")
+    y, core = col // 2, col % 2
+    xn = (1 - x, col, z)
+    yn = (x, (1 - y) * 2 + core, z)
+    sib = (x, y * 2 + 1 - core, z)
+    home = x == y
+    away = x != y
+    crow = pl.ds(pl.multiple_of(core * cw, cw), cw)
+    crow_sib = pl.ds(pl.multiple_of((1 - core) * cw, cw), cw)
+    own = pl.ds(pl.multiple_of(x * m, m), m)
+    oth = pl.ds(pl.multiple_of((1 - x) * m, m), m)
+
+    def group(t):
+        return lax.rem(z + 1 + t // gz, nz) * gz + lax.rem(t, gz)
+
+    def remote(src, dst, send, recv, dev):
+        return pltpu.make_async_remote_copy(
+            src_ref=src, dst_ref=dst, send_sem=send, recv_sem=recv, device_id=dev, device_id_type=MESH
+        )
+
+    def wait_oth(g):
+        remote(wv.at[g, :, crow, oth], wv.at[g, :, crow, oth], s2.at[g], r_oth.at[g], xn).wait_recv()
+
+    barrier = pltpu.get_barrier_semaphore()
+    others = [xn, yn, sib] + [(x, col, lax.rem(z + d, nz)) for d in range(1, nz)]
+    for dev in others:
+        pl.semaphore_signal(barrier, inc=1, device_id=dev, device_id_type=MESH)
+    pl.semaphore_wait(barrier, len(others))
+
+    def begin(t, carry):
+        g = group(t)
+        even = lax.rem(t, 2) == 0
+
+        @pl.when(home)
+        def _():
+            remote(w_ref.at[g], wv.at[g, :, crow, own], s1.at[g], r_own.at[g], yn).start()
+            pltpu.make_async_copy(w_ref.at[g], wv.at[g, :, crow, own], l_sem.at[g]).start()
+
+        @pl.when(jnp.logical_and(away, even))
+        def _():
+            remote(w_ref.at[g], wv.at[g, :, crow, own], s1.at[g], r_oth.at[g], xn).start()
+
+        @pl.when(jnp.logical_and(away, jnp.logical_not(even)))
+        def _():
+            remote(w_ref.at[g], st.at[g], s1.at[g], r_st.at[g], yn).start()
+
+        for j in range(nj):
+            pltpu.make_async_copy(
+                t_ref.at[g, j], tv.at[g, :, :, pl.ds(j * nb, nb)], t_sem.at[g, j]
+            ).start()
+        return carry
+
+    lax.fori_loop(0, ng, begin, 0)
+
+    def forward(t):
+        g = group(t)
+        even = lax.rem(t, 2) == 0
+
+        @pl.when(jnp.logical_and(home, jnp.logical_not(even)))
+        def _():
+            remote(st.at[g], st.at[g], s1.at[g], r_st.at[g], yn).wait_recv()
+            remote(st.at[g], wv.at[g, :, crow, own], s2.at[g], r_oth.at[g], xn).start()
+
+        @pl.when(home == even)
+        def _():
+            wait_oth(g)
+            remote(wv.at[g, :, crow, oth], wv.at[g, :, crow, oth], s2.at[g], r_oth.at[g], yn).start()
+
+    def share(t):
+        g = group(t)
+        even = lax.rem(t, 2) == 0
+
+        @pl.when(home != even)
+        def _():
+            wait_oth(g)
+
+        @pl.when(home)
+        def _():
+            pltpu.make_async_copy(w_ref.at[g], wv.at[g, :, crow, own], l_sem.at[g]).wait()
+
+        @pl.when(away)
+        def _():
+            remote(w_ref.at[g], wv.at[g, :, crow, own], s1.at[g], r_own.at[g], yn).wait_recv()
+
+        remote(wv.at[g, :, crow, :], wv.at[g, :, crow, :], sc.at[g], r_c.at[g], sib).start()
+
+    def product(g, lanes):
+        return lax.dot_general(
+            wv[g, :, :, lanes].reshape(depth, m),
+            tv[g].reshape(depth, n),
+            (((0,), (0,)), ((), ())),
+            preferred_element_type=jnp.float32,
+        )
+
+    def multiply(t):
+        g = group(t)
+        for j in range(nj):
+            pltpu.make_async_copy(
+                t_ref.at[g, j], tv.at[g, :, :, pl.ds(j * nb, nb)], t_sem.at[g, j]
+            ).wait()
+        remote(wv.at[g, :, crow, :], wv.at[g, :, crow_sib, :], sc.at[g], r_c.at[g], sib).wait_recv()
+        quantise(product(g, oth), xs.at[g])
+        remote(xs.at[g], xr.at[g], sx.at[g], r_x.at[g], xn).start()
+        pown[g] = product(g, own)
+
+    def owner(t):
+        return lax.rem(z + 1 + t // gz, nz)
+
+    def reduce(t):
+        g = group(t)
+        remote(xs.at[g], xr.at[g], sx.at[g], r_x.at[g], xn).wait_recv()
+        total = pown[g] + dequantise(xr.at[g])
+
+        @pl.when(t < ng - gz)
+        def _():
+            quantise(total, zs.at[g])
+            slot = lax.rem(t, gz)
+            remote(zs.at[g], zr.at[z, slot], sz.at[g], r_z.at[z, slot], (x, col, owner(t))).start()
+
+        @pl.when(t >= ng - gz)
+        def _():
+            o_ref[lax.rem(t, gz)] = total
+
+    def step(t, carry):
+        @pl.when(t < ng)
+        def _():
+            forward(t)
+
+        @pl.when(jnp.logical_and(t >= 1, t < ng + 1))
+        def _():
+            share(t - 1)
+            multiply(t - 1)
+
+        @pl.when(t >= 2)
+        def _():
+            reduce(t - 2)
+
+        return carry
+
+    lax.fori_loop(0, ng + 2, step, 0)
+
+    for d in range(nz - 1, 0, -1):
+        src = lax.rem(z + nz - d, nz)
+        for slot in range(gz):
+            remote(zr.at[src, slot], zr.at[src, slot], sz.at[0], r_z.at[src, slot], xn).wait_recv()
+            o_ref[slot] += dequantise(zr.at[src, slot])
+
+    def finish(t, carry):
+        g = group(t)
+        even = lax.rem(t, 2) == 0
+        remote(w_ref.at[g], st.at[g], s1.at[g], r_st.at[g], yn).wait_send()
+
+        @pl.when(jnp.logical_or(home, jnp.logical_not(even)))
+        def _():
+            remote(st.at[g], st.at[g], s2.at[g], r_oth.at[g], xn).wait_send()
+
+        remote(wv.at[g, :, crow, :], wv.at[g, :, crow, :], sc.at[g], r_c.at[g], sib).wait_send()
+        remote(xs.at[g], xr.at[g], sx.at[g], r_x.at[g], xn).wait_send()
+
+        @pl.when(t < ng - gz)
+        def _():
+            remote(zs.at[g], zs.at[g], sz.at[g], r_x.at[g], xn).wait_send()
+
+        return carry
+
+    lax.fori_loop(0, ng, finish, 0)
+
+
+def fused(masked, amplitudes):
+    ng, ni, nk, cw, na = masked.shape
+    nj, nb = amplitudes.shape[1], amplitudes.shape[4]
+    nz = lax.axis_size("rep")
+    m, n, gz = ni * na, nj * nb, ng // nz
+    w = jnp.transpose(masked, (0, 2, 3, 1, 4)).reshape(ng, nk, cw, m)
+    dma = pltpu.SemaphoreType.DMA
+    part = functools.partial
+    coded = (m + PAD, n)
+    return pl.pallas_call(
+        part(kernel, nz),
+        out_shape=jax.ShapeDtypeStruct((gz, m, n), jnp.float32),
+        in_specs=[pl.BlockSpec(memory_space=pl.ANY)] * 2,
+        out_specs=pl.BlockSpec(memory_space=pltpu.VMEM),
+        scratch_shapes=[
+            pltpu.VMEM((ng, nk, 2 * cw, 2 * m), jnp.bfloat16),
+            pltpu.VMEM((ng, nk, 2 * cw, n), jnp.bfloat16),
+            pltpu.VMEM((ng, nk, cw, m), jnp.bfloat16),
+            pltpu.VMEM((ng, m, n), jnp.float32),
+            pltpu.VMEM((ng,) + coded, jnp.int16),
+            pltpu.VMEM((ng,) + coded, jnp.int16),
+            pltpu.VMEM((ng,) + coded, jnp.int16),
+            pltpu.VMEM((nz, gz) + coded, jnp.int16),
+            dma((ng, nj)),
+        ]
+        + [dma((ng,))] * 11
+        + [dma((nz, gz))],
+        compiler_params=pltpu.CompilerParams(
+            collective_id=0, has_side_effects=True, vmem_limit_bytes=56 * 1024 * 1024
+        ),
+    )(w, amplitudes)
+
+
 def body(integrals, amplitudes, virt_count, occ_irrep):
-    ngroup = integrals.shape[0]
-    k_local = integrals.shape[2]
-    c_local = integrals.shape[3]
-    nvirt = integrals.shape[4]
+    ngroup, ni, k_local, c_local, nvirt = integrals.shape
+    nj = amplitudes.shape[1]
     rep_index = lax.axis_index("rep")
     col_index = lax.axis_index("col")
     occ_local = lax.dynamic_slice_in_dim(occ_irrep, rep_index * k_local, k_local)
@@ -33,8 +263,11 @@
     keep = c_live[:, None, :, :, None] & a_live[:, None, None, None, :]
     masked = jnp.where(keep, integrals, jnp.zeros_like(integrals))
     owned = ngroup // lax.axis_size("rep")
-    partial_cycle = contract(masked, amplitudes)
-    summed = lax.psum_scatter(partial_cycle, "rep", scatter_dimension=0, tiled=True)
+    if lax.axis_size("row") == 2 and lax.axis_size("col") == 4 and amplitudes.shape[3] == 2 * c_local:
+        summed = fused(masked, amplitudes).reshape(owned, ni, nvirt, nj, nvirt)
+    else:
+        partial_cycle = contract(masked, amplitudes)
+        summed = lax.psum_scatter(partial_cycle, "rep", scatter_dimension=0, tiled=True)
     own_counts = lax.dynamic_slice_in_dim(virt_count, rep_index * owned, owned)
     b_live = places[None, :] < own_counts[:, None]
     result = jnp.where(b_live[:, None, None, None, :], summed, jnp.zeros_like(summed))

time: 360 us -> 142 us (0.39)
  waiting for transfers between devices: 323 us -> 0 us
  Pallas kernels: 0 us -> 132 us
  matrix products: 14.3 us -> 0 us
  between operations: 13.2 us -> 0.03 us
    all_gather x2 -> x0, waiting for transfers between devices: 246 us -> none  [the longest x1 189 us: contract(): lax.all_gather(t_part, 'row', axis=3, tiled=True)]
    pallas_call x0 -> x1, Pallas kernels: none -> 132 us  [fused(): pl.pallas_call(part(kernel, nz), out_shape=jax.ShapeDtypeStruct((gz, m, n...]
    reduce_scatter x1 -> x0, waiting for transfers between devices: 76.8 us -> none  [body(): lax.psum_scatter(partial_cycle, 'rep', scatter_dimension=0, tiled=True)]
    dot_general x1 -> x0, matrix products: 14.3 us -> none  [contract(): jnp.einsum('gikca,gjkcb->giajb', w_full, lax.all_gather(t_part, 'row', ax...]
  transfers between devices with their start and end apart: 3 -> 0, of which waited for: 3 -> 0; matrix products, arithmetic and copies ran while one was open for 0% -> 0% of each run, Pallas kernels for 0% -> 0%
where the time goes in v1:
time: 142 us
  Pallas kernels  132 us (93%)
  other arithmetic  6.96 us (5%)
  local copies, waits for them, and re-layouts  2.8 us (2%)
    pallas_call x1, Pallas kernels, fused(): pl.pallas_call(part(kernel, nz), out_shape=jax.ShapeDtypeStruct((gz, m, n...  132 us
    reshape x1, other arithmetic, fused(): w = jnp.transpose(masked, (0, 2, 3, 1, 4)).reshape(ng, nk, cw, m)  3.53 us

profile of v1, /device:TPU:0, one launch (start us, length us, event | category | flops | bytes accessed | tf_op | source)
XLA Modules:
  0.0 142.0 jit_solution(10075083274626686991)
XLA Ops:
  0.0 0.7 dynamic_slice.6
  0.7 0.1 iota_compare_fusion.2
  0.8 0.7 dynamic_slice.7
  1.5 0.7 iota_compare_fusion.1
  2.3 0.7 select_reduce_fusion
  3.0 0.1 broadcast_compare_fusion
  3.1 0.8 broadcast_and_fusion
  3.9 3.5 %copy_bitcast_fusion.w_ref = bf16[8,15,32,256]{3,2,1,0:T(8,128)(2,1)} fusion(bf16[8,2,15,32,128]{4,3,2,1,0:T(8,128)(2,1)} %param.4, pred[8,15,32,128]{3,2,1,0:T(8,128)(4,1)S(1)} %broadcast_and_fusion), kind=kLoop, calls=%fused_computation | loop fusion | flops 983040 | bytes 4423680 | tf_op jit(solution)/shard_map/reshape | solution.py:221
  7.4 132.2 %shard_map.46 = f32[2,256,512]{2,1,0:T(8,128)} custom-call(bf16[8,15,32,256]{3,2,1,0:T(8,128)(2,1)} %copy_bitcast_fusion.w_ref, bf16[8,4,15,64,128]{4,3,2,1,0:T(8,128)(2,1)} %t_ref.1), custom_call_target="tpu_custom_call" | custom-call | tf_op jit(solution)/shard_map/pallas_call | solution.py:225
  139.7 1.3 reshape.72
  141.0 1.0 select_convert_fusion
  (2 shorter events, 0.0 us)

commit v2 on v1

--- a/solution.py
+++ b/solution.py
@@ -10,6 +10,7 @@
 MESH = pl.DeviceIdType.MESH
 TOP = 32767.0
 PAD = 16
+AHEAD = 2
 
 
 def contract(w_part, t_part):
@@ -38,9 +39,10 @@
     return ref[0:rows, :].astype(jnp.int32).astype(jnp.float32) * (jnp.exp2(code * 0.125) * (1.0 / TOP))
 
 
-def kernel(nz, w_ref, t_ref, o_ref, wv, tv, st, pown, xs, xr, zs, zr,
+def kernel(nz, count_ref, occ_ref, w_ref, t_ref, o_ref, wv, wm, tv, st, pown, xs, xr, zs, zr,
            t_sem, l_sem, s1, s2, sc, sx, sz, r_own, r_oth, r_st, r_c, r_x, r_z):
-    ng, nk, cw, m = w_ref.shape
+    ng, ni, nk, cw, na = w_ref.shape
+    m = ni * na
     nj, nb = t_ref.shape[1], t_ref.shape[4]
     n = nj * nb
     depth = nk * 2 * cw
@@ -74,30 +76,36 @@
         pl.semaphore_signal(barrier, inc=1, device_id=dev, device_id_type=MESH)
     pl.semaphore_wait(barrier, len(others))
 
-    def begin(t, carry):
+    def pieces(g, dst, send, recv, dev):
+        for i in range(ni):
+            remote(w_ref.at[g, i], dst.at[:, :, pl.ds(i * na, na)], send, recv, dev).start()
+
+    def begin(t):
         g = group(t)
         even = lax.rem(t, 2) == 0
+        mine = wv.at[g, :, crow, own]
 
         @pl.when(home)
         def _():
-            remote(w_ref.at[g], wv.at[g, :, crow, own], s1.at[g], r_own.at[g], yn).start()
-            pltpu.make_async_copy(w_ref.at[g], wv.at[g, :, crow, own], l_sem.at[g]).start()
+            pieces(g, mine, s1.at[g], r_own.at[g], yn)
+            for i in range(ni):
+                pltpu.make_async_copy(w_ref.at[g, i], mine.at[:, :, pl.ds(i * na, na)], l_sem.at[g]).start()
 
         @pl.when(jnp.logical_and(away, even))
         def _():
-            remote(w_ref.at[g], wv.at[g, :, crow, own], s1.at[g], r_oth.at[g], xn).start()
+            pieces(g, mine, s1.at[g], r_oth.at[g], xn)
 
         @pl.when(jnp.logical_and(away, jnp.logical_not(even)))
         def _():
-            remote(w_ref.at[g], st.at[g], s1.at[g], r_st.at[g], yn).start()
+            pieces(g, st.at[g], s1.at[g], r_st.at[g], yn)
 
         for j in range(nj):
             pltpu.make_async_copy(
                 t_ref.at[g, j], tv.at[g, :, :, pl.ds(j * nb, nb)], t_sem.at[g, j]
             ).start()
-        return carry
-
-    lax.fori_loop(0, ng, begin, 0)
+
+    for t in range(AHEAD):
+        begin(t)
 
     def forward(t):
         g = group(t)
@@ -108,11 +116,19 @@
             remote(st.at[g], st.at[g], s1.at[g], r_st.at[g], yn).wait_recv()
             remote(st.at[g], wv.at[g, :, crow, own], s2.at[g], r_oth.at[g], xn).start()
 
-        @pl.when(home == even)
+        @pl.when(jnp.logical_and(home, even))
         def _():
             wait_oth(g)
             remote(wv.at[g, :, crow, oth], wv.at[g, :, crow, oth], s2.at[g], r_oth.at[g], yn).start()
 
+    def onward(t):
+        g = group(t)
+
+        @pl.when(jnp.logical_and(away, lax.rem(t, 2) == 1))
+        def _():
+            wait_oth(g)
+            remote(wv.at[g, :, crow, oth], wv.at[g, :, crow, oth], s2.at[g], r_oth.at[g], yn).start()
+
     def share(t):
         g = group(t)
         even = lax.rem(t, 2) == 0
@@ -123,17 +139,17 @@
 
         @pl.when(home)
         def _():
-            pltpu.make_async_copy(w_ref.at[g], wv.at[g, :, crow, own], l_sem.at[g]).wait()
+            pltpu.make_async_copy(st.at[g], wv.at[g, :, crow, own], l_sem.at[g]).wait()
 
         @pl.when(away)
         def _():
-            remote(w_ref.at[g], wv.at[g, :, crow, own], s1.at[g], r_own.at[g], yn).wait_recv()
+            remote(st.at[g], wv.at[g, :, crow, own], s1.at[g], r_own.at[g], yn).wait_recv()
 
         remote(wv.at[g, :, crow, :], wv.at[g, :, crow, :], sc.at[g], r_c.at[g], sib).start()
 
     def product(g, lanes):
         return lax.dot_general(
-            wv[g, :, :, lanes].reshape(depth, m),
+            wm[:, :, lanes].reshape(depth, m),
             tv[g].reshape(depth, n),
             (((0,), (0,)), ((), ())),
             preferred_element_type=jnp.float32,
@@ -146,6 +162,12 @@
                 t_ref.at[g, j], tv.at[g, :, :, pl.ds(j * nb, nb)], t_sem.at[g, j]
             ).wait()
         remote(wv.at[g, :, crow, :], wv.at[g, :, crow_sib, :], sc.at[g], r_c.at[g], sib).wait_recv()
+        rows = x * (2 * cw) + lax.broadcasted_iota(jnp.int32, (2 * cw, 2 * m), 0)
+        a_live = lax.rem(lax.broadcasted_iota(jnp.int32, (2 * cw, 2 * m), 1), na) < count_ref[g]
+        for k in range(nk):
+            limit = count_ref[jnp.bitwise_xor(g, occ_ref[z * nk + k])]
+            keep = jnp.where(jnp.logical_and(a_live, rows < limit), 1.0, 0.0).astype(jnp.bfloat16)
+            wm[k] = wv[g, k] * keep
         quantise(product(g, oth), xs.at[g])
         remote(xs.at[g], xr.at[g], sx.at[g], r_x.at[g], xn).start()
         pown[g] = product(g, own)
@@ -175,16 +197,24 @@
 
         @pl.when(jnp.logical_and(t >= 1, t < ng + 1))
         def _():
-            share(t - 1)
-            multiply(t - 1)
-
-        @pl.when(t >= 2)
-        def _():
-            reduce(t - 2)
+            onward(t - 1)
+
+        @pl.when(t < ng - AHEAD)
+        def _():
+            begin(t + AHEAD)
+
+        @pl.when(jnp.logical_and(t >= 2, t < ng + 2))
+        def _():
+            share(t - 2)
+            multiply(t - 2)
+
+        @pl.when(t >= 3)
+        def _():
+            reduce(t - 3)
 
         return carry
 
-    lax.fori_loop(0, ng + 2, step, 0)
+    lax.fori_loop(0, ng + 3, step, 0)
 
     for d in range(nz - 1, 0, -1):
         src = lax.rem(z + nz - d, nz)
@@ -195,7 +225,7 @@
     def finish(t, carry):
         g = group(t)
         even = lax.rem(t, 2) == 0
-        remote(w_ref.at[g], st.at[g], s1.at[g], r_st.at[g], yn).wait_send()
+        remote(st.at[g], st.at[g], s1.at[g], r_st.at[g], yn).wait_send()
 
         @pl.when(jnp.logical_or(home, jnp.logical_not(even)))
         def _():
@@ -213,22 +243,22 @@
     lax.fori_loop(0, ng, finish, 0)
 
 
-def fused(masked, amplitudes):
-    ng, ni, nk, cw, na = masked.shape
+def fused(integrals, amplitudes, virt_count, occ_irrep):
+    ng, ni, nk, cw, na = integrals.shape
     nj, nb = amplitudes.shape[1], amplitudes.shape[4]
     nz = lax.axis_size("rep")
     m, n, gz = ni * na, nj * nb, ng // nz
-    w = jnp.transpose(masked, (0, 2, 3, 1, 4)).reshape(ng, nk, cw, m)
     dma = pltpu.SemaphoreType.DMA
     part = functools.partial
     coded = (m + PAD, n)
     return pl.pallas_call(
         part(kernel, nz),
         out_shape=jax.ShapeDtypeStruct((gz, m, n), jnp.float32),
-        in_specs=[pl.BlockSpec(memory_space=pl.ANY)] * 2,
+        in_specs=[pl.BlockSpec(memory_space=pltpu.SMEM)] * 2 + [pl.BlockSpec(memory_space=pl.ANY)] * 2,
         out_specs=pl.BlockSpec(memory_space=pltpu.VMEM),
         scratch_shapes=[
             pltpu.VMEM((ng, nk, 2 * cw, 2 * m), jnp.bfloat16),
+            pltpu.VMEM((nk, 2 * cw, 2 * m), jnp.bfloat16),
             pltpu.VMEM((ng, nk, 2 * cw, n), jnp.bfloat16),
             pltpu.VMEM((ng, nk, cw, m), jnp.bfloat16),
             pltpu.VMEM((ng, m, n), jnp.float32),
@@ -243,33 +273,36 @@
         compiler_params=pltpu.CompilerParams(
             collective_id=0, has_side_effects=True, vmem_limit_bytes=56 * 1024 * 1024
         ),
-    )(w, amplitudes)
-
-
-def body(integrals, amplitudes, virt_count, occ_irrep):
-    ngroup, ni, k_local, c_local, nvirt = integrals.shape
-    nj = amplitudes.shape[1]
-    rep_index = lax.axis_index("rep")
-    col_index = lax.axis_index("col")
-    occ_local = lax.dynamic_slice_in_dim(occ_irrep, rep_index * k_local, k_local)
+    )(virt_count, occ_irrep, integrals, amplitudes)
+
+
+def gathered(integrals, amplitudes, virt_count, occ_irrep):
+    ngroup, _, k_local, c_local, nvirt = integrals.shape
+    occ_local = lax.dynamic_slice_in_dim(occ_irrep, lax.axis_index("rep") * k_local, k_local)
     groups = jnp.arange(ngroup, dtype=jnp.int32)
     blocks = jnp.bitwise_xor(groups[:, None], occ_local[None, :])
     onehot = blocks[:, :, None] == groups[None, None, :]
     limit = jnp.sum(jnp.where(onehot, virt_count[None, None, :], 0), axis=2)
-    c_global = col_index * c_local + jnp.arange(c_local, dtype=jnp.int32)
+    c_global = lax.axis_index("col") * c_local + jnp.arange(c_local, dtype=jnp.int32)
     c_live = c_global[None, None, :] < limit[:, :, None]
-    places = jnp.arange(nvirt, dtype=jnp.int32)
-    a_live = places[None, :] < virt_count[:, None]
+    a_live = jnp.arange(nvirt, dtype=jnp.int32)[None, :] < virt_count[:, None]
     keep = c_live[:, None, :, :, None] & a_live[:, None, None, None, :]
     masked = jnp.where(keep, integrals, jnp.zeros_like(integrals))
+    partial_cycle = contract(masked, amplitudes)
+    return lax.psum_scatter(partial_cycle, "rep", scatter_dimension=0, tiled=True)
+
+
+def body(integrals, amplitudes, virt_count, occ_irrep):
+    ngroup, ni, _, c_local, nvirt = integrals.shape
+    nj = amplitudes.shape[1]
     owned = ngroup // lax.axis_size("rep")
     if lax.axis_size("row") == 2 and lax.axis_size("col") == 4 and amplitudes.shape[3] == 2 * c_local:
-        summed = fused(masked, amplitudes).reshape(owned, ni, nvirt, nj, nvirt)
+        summed = fused(integrals, amplitudes, virt_count, occ_irrep)
+        summed = summed.reshape(owned, ni, nvirt, nj, nvirt)
     else:
-        partial_cycle = contract(masked, amplitudes)
-        summed = lax.psum_scatter(partial_cycle, "rep", scatter_dimension=0, tiled=True)
-    own_counts = lax.dynamic_slice_in_dim(virt_count, rep_index * owned, owned)
-    b_live = places[None, :] < own_counts[:, None]
+        summed = gathered(integrals, amplitudes, virt_count, occ_irrep)
+    own_counts = lax.dynamic_slice_in_dim(virt_count, lax.axis_index("rep") * owned, owned)
+    b_live = jnp.arange(nvirt, dtype=jnp.int32)[None, :] < own_counts[:, None]
     result = jnp.where(b_live[:, None, None, None, :], summed, jnp.zeros_like(summed))
     return result.astype(jnp.bfloat16)
 

time: 142 us -> 94.2 us (0.66)
  Pallas kernels: 132 us -> 91.5 us
  other arithmetic: 6.96 us -> 1.1 us
    pallas_call x1, Pallas kernels: 132 us -> 91.5 us  [fused(): pl.pallas_call(part(kernel, nz), out_shape=jax.ShapeDtypeStruct((gz, m, n...]
    reshape x1 -> x0, other arithmetic: 3.53 us -> none  [fused(): w = jnp.transpose(masked, (0, 2, 3, 1, 4)).reshape(ng, nk, cw, m)]
where the time goes in v2:
time: 94.2 us; the launch traced here: 94 us
  Pallas kernels  91.5 us (97%)
  local copies, waits for them, and re-layouts  1.43 us (2%)
  other arithmetic  1.1 us (1%)
    pallas_call x1, Pallas kernels, fused(): pl.pallas_call(part(kernel, nz), out_shape=jax.ShapeDtypeStruct((gz, m, n...  91.5 us

profile of v2, /device:TPU:0, one launch (start us, length us, event | category | flops | bytes accessed | tf_op | source)
XLA Modules:
  0.0 94.0 jit_solution(13599829872341905426)
XLA Ops:
  0.0 0.0 copy-start
  0.0 91.5 %shard_map.46 = f32[2,256,512]{2,1,0:T(8,128)} custom-call(s32[8]{0:T(128)} %count_ref.1, s32[60]{0:T(128)} %occ_ref.1, bf16[8,2,15,32,128]{4,3,2,1,0:T(8,128)(2,1)} %w_ref.1, bf16[8,4,15,64,128]{4,3,2,1,0:T(8,128)(2,1)} %t_ref.1), custom_call_target="tpu_custom_call" | custom-call | tf_op jit(solution)/shard_map/pallas_call | solution.py:254
  91.5 1.3 %reshape.20 = bf16[2,2,128,4,128]{4,3,2,1,0:T(4,128)(2,1)S(1)} reshape(f32[2,256,512]{2,1,0:T(8,128)} %shard_map.46) | data formatting | bytes 1572864 | tf_op jit(solution)/shard_map/reshape | solution.py:301
  92.9 0.0 copy-done
  92.9 0.1 dynamic_slice.3
  92.9 0.1 iota_compare_fusion
  93.0 1.0 %select_convert_fusion = bf16[2,2,128,4,128]{4,3,2,1,0:T(4,128)(2,1)} fusion(bf16[2,2,128,4,128]{4,3,2,1,0:T(4,128)(2,1)S(1)} %reshape.20, pred[2,128]{1,0:T(4,128)(4,1)S(1)} %iota_compare_fusion), kind=kLoop, calls=%fused_computation | loop fusion | flops 262144 | bytes 1048832 | tf_op jit(solution)/shard_map/convert_element_type | solution.py:307
Async XLA Ops:
  0.0 92.9 %copy-start = (s32[8]{0:T(128)S(1)}, s32[8]{0:T(128)}, u32[]{:S(2)}) copy-start(s32[8]{0:T(128)} %count_ref.1) | copy-start | bytes 100

commit v3 on v2

--- a/solution.py
+++ b/solution.py
@@ -188,7 +188,13 @@
 
         @pl.when(t >= ng - gz)
         def _():
-            o_ref[lax.rem(t, gz)] = total
+            o_ref[lax.rem(t, gz)] += total
+
+    def collect(t):
+        src = lax.rem(z + nz - 1 - t // gz, nz)
+        slot = lax.rem(t, gz)
+        remote(zr.at[src, slot], zr.at[src, slot], sz.at[0], r_z.at[src, slot], xn).wait_recv()
+        o_ref[slot] += dequantise(zr.at[src, slot])
 
     def step(t, carry):
         @pl.when(t < ng)
@@ -206,21 +212,23 @@
         @pl.when(jnp.logical_and(t >= 2, t < ng + 2))
         def _():
             share(t - 2)
+
+        @pl.when(t >= 3)
+        def _():
+            reduce(t - 3)
+
+        @pl.when(t >= 3 + gz)
+        def _():
+            collect(t - 3 - gz)
+
+        @pl.when(jnp.logical_and(t >= 2, t < ng + 2))
+        def _():
             multiply(t - 2)
 
-        @pl.when(t >= 3)
-        def _():
-            reduce(t - 3)
-
         return carry
 
+    o_ref[...] = jnp.zeros_like(o_ref)
     lax.fori_loop(0, ng + 3, step, 0)
-
-    for d in range(nz - 1, 0, -1):
-        src = lax.rem(z + nz - d, nz)
-        for slot in range(gz):
-            remote(zr.at[src, slot], zr.at[src, slot], sz.at[0], r_z.at[src, slot], xn).wait_recv()
-            o_ref[slot] += dequantise(zr.at[src, slot])
 
     def finish(t, carry):
         g = group(t)

time: 94.2 us -> 109 us (1.16)
  the two profiles are of different devices: /device:TPU:0 before, /device:TPU:25 now
where the time goes in v3:
time: 109 us
  Pallas kernels  106 us (97%)
  local copies, waits for them, and re-layouts  1.43 us (1%)
  other arithmetic  1.1 us (1%)
    pallas_call x1, Pallas kernels, fused(): pl.pallas_call(part(kernel, nz), out_shape=jax.ShapeDtypeStruct((gz, m, n...  106 us

profile of v3, /device:TPU:25, one launch (start us, length us, event | category | flops | bytes accessed | tf_op | source)
XLA Modules:
  0.0 109.0 jit_solution(10533967201879344453)
XLA Ops:
  0.0 0.0 copy-start
  0.0 106.5 %shard_map.46 = f32[2,256,512]{2,1,0:T(8,128)} custom-call(s32[8]{0:T(128)} %count_ref.1, s32[60]{0:T(128)} %occ_ref.1, bf16[8,2,15,32,128]{4,3,2,1,0:T(8,128)(2,1)} %w_ref.1, bf16[8,4,15,64,128]{4,3,2,1,0:T(8,128)(2,1)} %t_ref.1), custom_call_target="tpu_custom_call" | custom-call | tf_op jit(solution)/shard_map/pallas_call | solution.py:262
  106.5 1.3 %reshape.20 = bf16[2,2,128,4,128]{4,3,2,1,0:T(4,128)(2,1)S(1)} reshape(f32[2,256,512]{2,1,0:T(8,128)} %shard_map.46) | data formatting | bytes 1572864 | tf_op jit(solution)/shard_map/reshape | solution.py:309
  107.8 0.0 copy-done
  107.8 0.1 dynamic_slice.3
  107.9 0.1 iota_compare_fusion
  108.0 1.0 select_convert_fusion
Async XLA Ops:
  0.0 107.8 %copy-start = (s32[8]{0:T(128)S(1)}, s32[8]{0:T(128)}, u32[]{:S(2)}) copy-start(s32[8]{0:T(128)} %count_ref.1) | copy-start | bytes 100

commit v4 on v3

--- a/solution.py
+++ b/solution.py
@@ -11,6 +11,7 @@
 TOP = 32767.0
 PAD = 16
 AHEAD = 2
+LAG = 4
 
 
 def contract(w_part, t_part):
@@ -213,22 +214,22 @@
         def _():
             share(t - 2)
 
-        @pl.when(t >= 3)
-        def _():
-            reduce(t - 3)
-
-        @pl.when(t >= 3 + gz)
-        def _():
-            collect(t - 3 - gz)
+        @pl.when(t >= LAG + gz)
+        def _():
+            collect(t - LAG - gz)
 
         @pl.when(jnp.logical_and(t >= 2, t < ng + 2))
         def _():
             multiply(t - 2)
 
+        @pl.when(t >= LAG)
+        def _():
+            reduce(t - LAG)
+
         return carry
 
     o_ref[...] = jnp.zeros_like(o_ref)
-    lax.fori_loop(0, ng + 3, step, 0)
+    lax.fori_loop(0, ng + LAG, step, 0)
 
     def finish(t, carry):
         g = group(t)

time: 109 us -> 108 us (level)
  the two profiles are of different devices: /device:TPU:25 before, /device:TPU:19 now
where the time goes in v4:
time: 108 us
  Pallas kernels  106 us (98%)
  local copies, waits for them, and re-layouts  1.43 us (1%)
  other arithmetic  1.1 us (1%)
    pallas_call x1, Pallas kernels, fused(): pl.pallas_call(part(kernel, nz), out_shape=jax.ShapeDtypeStruct((gz, m, n...  106 us

profile of v4, /device:TPU:19, one launch (start us, length us, event | category | flops | bytes accessed | tf_op | source)
XLA Modules:
  0.0 108.3 jit_solution(8632280270389672578)
XLA Ops:
  0.0 0.0 copy-start
  0.0 105.7 %shard_map.46 = f32[2,256,512]{2,1,0:T(8,128)} custom-call(s32[8]{0:T(128)} %count_ref.1, s32[60]{0:T(128)} %occ_ref.1, bf16[8,2,15,32,128]{4,3,2,1,0:T(8,128)(2,1)} %w_ref.1, bf16[8,4,15,64,128]{4,3,2,1,0:T(8,128)(2,1)} %t_ref.1), custom_call_target="tpu_custom_call" | custom-call | tf_op jit(solution)/shard_map/pallas_call | solution.py:263
  105.7 1.3 %reshape.20 = bf16[2,2,128,4,128]{4,3,2,1,0:T(4,128)(2,1)S(1)} reshape(f32[2,256,512]{2,1,0:T(8,128)} %shard_map.46) | data formatting | bytes 1572864 | tf_op jit(solution)/shard_map/reshape | solution.py:310
  107.1 0.0 copy-done
  107.1 0.1 dynamic_slice.3
  107.2 0.1 iota_compare_fusion
  107.3 1.0 select_convert_fusion
Async XLA Ops:
  0.0 107.1 %copy-start = (s32[8]{0:T(128)S(1)}, s32[8]{0:T(128)}, u32[]{:S(2)}) copy-start(s32[8]{0:T(128)} %count_ref.1) | copy-start | bytes 100

commit v5 on v4

--- a/solution.py
+++ b/solution.py
@@ -11,7 +11,8 @@
 TOP = 32767.0
 PAD = 16
 AHEAD = 2
-LAG = 4
+LAG = 3
+SLACK = 4
 
 
 def contract(w_part, t_part):
@@ -214,10 +215,6 @@
         def _():
             share(t - 2)
 
-        @pl.when(t >= LAG + gz)
-        def _():
-            collect(t - LAG - gz)
-
         @pl.when(jnp.logical_and(t >= 2, t < ng + 2))
         def _():
             multiply(t - 2)
@@ -225,11 +222,21 @@
         @pl.when(t >= LAG)
         def _():
             reduce(t - LAG)
+
+        @pl.when(t >= LAG + SLACK)
+        def _():
+            collect(t - LAG - SLACK)
 
         return carry
 
     o_ref[...] = jnp.zeros_like(o_ref)
     lax.fori_loop(0, ng + LAG, step, 0)
+
+    def rest(t, carry):
+        collect(t)
+        return carry
+
+    lax.fori_loop(ng - SLACK, ng - gz, rest, 0)
 
     def finish(t, carry):
         g = group(t)

time: 108 us -> 93.9 us (0.87)
  the two profiles are of different devices: /device:TPU:19 before, /device:TPU:0 now
where the time goes in v5:
time: 93.9 us; the launch traced here: 93.7 us
  Pallas kernels  91.2 us (97%)
  local copies, waits for them, and re-layouts  1.43 us (2%)
  other arithmetic  1.1 us (1%)
    pallas_call x1, Pallas kernels, fused(): pl.pallas_call(part(kernel, nz), out_shape=jax.ShapeDtypeStruct((gz, m, n...  91.2 us

profile of v5, /device:TPU:0, one launch (start us, length us, event | category | flops | bytes accessed | tf_op | source)
XLA Modules:
  0.0 93.7 jit_solution(4989213569136413475)
XLA Ops:
  0.0 0.0 copy-start
  0.0 91.2 %shard_map.46 = f32[2,256,512]{2,1,0:T(8,128)} custom-call(s32[8]{0:T(128)} %count_ref.1, s32[60]{0:T(128)} %occ_ref.1, bf16[8,2,15,32,128]{4,3,2,1,0:T(8,128)(2,1)} %w_ref.1, bf16[8,4,15,64,128]{4,3,2,1,0:T(8,128)(2,1)} %t_ref.1), custom_call_target="tpu_custom_call" | custom-call | tf_op jit(solution)/shard_map/pallas_call | solution.py:270
  91.2 1.3 %reshape.20 = bf16[2,2,128,4,128]{4,3,2,1,0:T(4,128)(2,1)S(1)} reshape(f32[2,256,512]{2,1,0:T(8,128)} %shard_map.46) | data formatting | bytes 1572864 | tf_op jit(solution)/shard_map/reshape | solution.py:317
  92.6 0.0 copy-done
  92.6 0.1 dynamic_slice.3
  92.6 0.1 iota_compare_fusion
  92.7 1.0 %select_convert_fusion = bf16[2,2,128,4,128]{4,3,2,1,0:T(4,128)(2,1)} fusion(bf16[2,2,128,4,128]{4,3,2,1,0:T(4,128)(2,1)S(1)} %reshape.20, pred[2,128]{1,0:T(4,128)(4,1)S(1)} %iota_compare_fusion), kind=kLoop, calls=%fused_computation | loop fusion | flops 262144 | bytes 1048832 | tf_op jit(solution)/shard_map/convert_element_type | solution.py:323
Async XLA Ops:
  0.0 92.6 %copy-start = (s32[8]{0:T(128)S(1)}, s32[8]{0:T(128)}, u32[]{:S(2)}) copy-start(s32[8]{0:T(128)} %count_ref.1) | copy-start | bytes 100
